TPU v7x, 32 devices: a whole 2x2x4 slice. The times are simulated.
32 devices in a mesh: dp: 8 (over z, x), bank: 4 (over y, core).
Axes of the slice: x: 2, y: 2, z: 4, core: 2. Of those that a mesh axis runs over, the one named last changes fastest.
Arguments:
- features: float32 [128, 128], P('dp'), may hold values from -6 to 6
- video_ids: int32 [8, 16], P('dp'), may hold values from 0 to 4, never falling along the last dimension, each value on 1 to 8 neighbouring positions
- bank: float32 [16384, 128], P(('dp', 'bank')), may hold values from -6 to 6
- loss_weight: float32 [128], P('dp'), may hold values from 0.5 to 2
Outputs:
- loss: float32 [128], P('dp')
- feature_grad: float32 [128, 128], P('dp')
Inputs may be any that keep to these rules, and one draw needn't show every extreme that they name: `video_ids`: each row of 16 frames holds 5 videos as runs of equal ids in ascending order, each video 1 to 8 frames and one exactly 8.
All inputs are finite; a program needn't handle non-finite values.
Results may differ from a plain program's by a relative error of at most 0.0003.
Values sent between devices are 32-bit elements; how exact they have to be, the bound alone decides.
A program may use at most 64 MiB of HBM per device.

v0:
```python
import math
import jax
import jax.numpy as jnp
from jax import lax
from jax.sharding import PartitionSpec as P

EPSILON = 1e-06
TAU_BACK = 0.1
HIGHEST = lax.Precision.HIGHEST


def unit_rows(values):
    return values / jnp.sqrt(jnp.sum(values * values, axis=1, keepdims=True) + EPSILON)


def cycle_loss(neighbour, normed, videos):
    frames = videos.shape[0]
    same_video = videos[:, None] == videos[None, :]
    row_index = lax.broadcasted_iota(jnp.int32, (frames, frames), 0)
    col_index = lax.broadcasted_iota(jnp.int32, (frames, frames), 1)
    earlier = same_video & (col_index < row_index)
    position = jnp.sum(jnp.where(earlier, 1.0, 0.0), axis=1).astype(neighbour.dtype)
    products = jnp.dot(neighbour, normed.T, precision=HIGHEST)
    distance = (
        jnp.sum(neighbour * neighbour, axis=1)[:, None]
        - 2.0 * products
        + jnp.sum(normed * normed, axis=1)[None, :]
    )
    back_weight = jnp.where(same_video, jnp.exp(-distance / TAU_BACK), 0.0)
    back_weight = back_weight / jnp.sum(back_weight, axis=1, keepdims=True)
    mean_pos = jnp.dot(back_weight, position, precision=HIGHEST)
    square_pos = jnp.dot(back_weight, position * position, precision=HIGHEST)
    spread = jnp.maximum(square_pos - mean_pos * mean_pos, 1.0)
    return (position - mean_pos) ** 2 / spread + 0.5 * jnp.log(spread)


def reduce_owner(partials):
    whole = lax.psum(partials, "bank")
    return lax.psum_scatter(whole, "dp", scatter_dimension=0, tiled=True)


def shards(features, video_ids, bank, loss_weight):
    per_owner, width = features.shape
    owners = lax.axis_size("dp")
    sharpness = 3.0 * math.sqrt(width)
    lengths = jnp.sqrt(jnp.sum(features * features, axis=1, keepdims=True) + EPSILON)
    normed = features / lengths
    keys = unit_rows(bank)
    gathered = lax.all_gather(normed, "dp", axis=0, tiled=True)
    group = 1
    while owners % (group * 2) == 0 and per_owner * group * 2 <= 512:
        group = group * 2
    step_rows = per_owner * group
    query_blocks = gathered.reshape(-1, step_rows, width)

    def forward_block(query_block):
        exp_scores = jnp.exp(sharpness * jnp.dot(query_block, keys.T, precision=HIGHEST))
        return (jnp.dot(exp_scores, keys, precision=HIGHEST), jnp.sum(exp_scores, axis=1))

    summed, partition = lax.map(forward_block, query_blocks)
    summed, partition = reduce_owner((summed.reshape(-1, width), partition.reshape(-1)))
    neighbour = summed / partition[:, None]
    loss, pullback = jax.vjp(
        lambda soft_rows, unit_part: cycle_loss(soft_rows, unit_part, video_ids[0]),
        neighbour,
        normed,
    )
    grad_soft, grad_local = pullback(loss_weight)
    gathered_grad = lax.all_gather(grad_soft, "dp", axis=0, tiled=True)
    grad_blocks = gathered_grad.reshape(-1, step_rows, width)

    def backward_block(paired):
        query_block, grad_block = paired
        exp_scores = jnp.exp(sharpness * jnp.dot(query_block, keys.T, precision=HIGHEST))
        projected = jnp.dot(grad_block, keys.T, precision=HIGHEST)
        return jnp.dot(exp_scores * projected, keys, precision=HIGHEST)

    moment = lax.map(backward_block, (query_blocks, grad_blocks)).reshape(-1, width)
    moment = reduce_owner((moment,))[0]
    along = jnp.sum(grad_soft * neighbour, axis=1, keepdims=True)
    grad_unit = grad_local + sharpness * (moment / partition[:, None] - along * neighbour)
    feature_grad = (
        grad_unit - normed * jnp.sum(normed * grad_unit, axis=1, keepdims=True)
    ) / lengths
    return (loss, feature_grad)


def solution(mesh):
    return jax.shard_map(
        shards,
        mesh=mesh,
        in_specs=(P("dp", None), P("dp", None), P(("dp", "bank"), None), P("dp")),
        out_specs=(P("dp"), P("dp", None)),
        check_vma=False,
    )
```

profile of v0, /device:TPU:0, one launch (start us, length us, event | category | flops | bytes accessed | tf_op | source)
XLA Modules:
  0.0 221.4 jit_solution(16359548754769475887)
XLA Ops:
  7.2 0.0 copy-start
  7.2 0.0 reduce-scatter.3.cloned.1.call-start
  7.2 0.8 multiply_reduce_fusion.6
  8.1 0.0 copy-start.1
  8.1 1.1 multiply_reduce_fusion
  9.2 0.0 copy-done.1
  9.2 0.2 multiply_reduce_fusion.4
  9.4 32.3 %all_gather.6 = f32[128,128]{1,0:T(8,128)S(1)} all-gather(f32[16,128]{1,0:T(8,128)S(1)} %get-tuple-element.42), channel_id=1, replica_groups=mesh['dp'=8,'bank'=4] {'dp'}, dimensions={0}, use_global_device_ids=true | all-gather | bytes 73728 | tf_op jit(solution)/shard_map/all_gather | solution.py:49
  41.7 0.0 copy-done
  41.7 0.6 fusion.28
  42.3 1.1 fusion.25
  43.4 0.0 reduce-scatter.3.cloned.1.call-update
  43.4 0.0 reduce-scatter.5.cloned.1.call-start
  43.5 0.0 copy-start.4
  43.5 0.6 copy-done.4
  44.1 0.6 dynamic-slice.2
  45.3 21.3 %all-reduce = f32[128]{0:T(128)S(1)} all-reduce(f32[128]{0:T(128)S(1)} %get-tuple-element.45), channel_id=3, replica_groups=mesh['dp'=8,'bank'=4] {'dp'}, use_global_device_ids=true, to_apply=%region_7.8.clone | all-reduce | flops 128 | bytes 1024
  66.7 0.1 dynamic-slice.3
  66.7 39.0 %reduce-scatter.3.cloned.1.call-done = f32[16,128]{1,0:T(8,128)} async-done(((f32[128,128]{1,0:T(8,128)}), f32[16,128]{1,0:T(8,128)}) %reduce-scatter.3.cloned.1.call-update) | async-done | bytes 8208 | tf_op jit(solution)/shard_map/reduce_scatter | solution.py:39
  105.7 6.0 %all-reduce.1 = (f32[16,128]{1,0:T(8,128)S(1)}, f32[16]{0:T(128)S(1)}) all-reduce(f32[16,128]{1,0:T(8,128)} %reduce-scatter.3.cloned.1.call-done, f32[16]{0:T(128)S(1)} %dynamic-slice.3), channel_id=1, replica_groups=mesh['dp'=8,'bank'=4] {'bank'}, use_global_device_ids=true, to_apply=%region_3.0 | all-reduce | flops 2064 | bytes 16512 | tf_op jit(solution)/shard_map/psum | solution.py:38
  111.7 0.2 multiply_reduce_fusion.5
  111.9 0.0 copy-start.2
  111.9 0.7 copy-done.2
  112.6 0.2 fusion.12
  112.8 0.0 copy-start.3
  112.8 0.2 convolution_bitcast_fusion.1
  113.0 0.5 copy-done.3
  113.5 0.7 add_add_fusion
  114.2 0.1 multiply_reduce_fusion.3
  114.3 0.2 multiply_reduce_fusion.8
  114.5 0.3 multiply_reduce_fusion.2
  114.8 30.5 %all_gather.7 = f32[128,128]{1,0:T(8,128)S(1)} all-gather(f32[16,128]{1,0:T(8,128)S(1)} %get-tuple-element.49), channel_id=1, replica_groups=mesh['dp'=8,'bank'=4] {'dp'}, dimensions={0}, use_global_device_ids=true | all-gather | bytes 73728 | tf_op jit(solution)/shard_map/all_gather | solution.py:69
  145.3 0.5 convolution_multiply_fusion
  145.8 1.1 fusion.24
  146.9 0.0 reduce-scatter.5.cloned.1.call-update
  147.0 60.8 %reduce-scatter.5.cloned.1.call-done = f32[16,128]{1,0:T(8,128)} async-done(((f32[128,128]{1,0:T(8,128)}), f32[16,128]{1,0:T(8,128)}) %reduce-scatter.5.cloned.1.call-update) | async-done | bytes 8208 | tf_op jit(solution)/shard_map/reduce_scatter | solution.py:39
  207.7 5.9 %psum.26 = f32[16,128]{1,0:T(8,128)S(1)} all-reduce(f32[16,128]{1,0:T(8,128)} %reduce-scatter.5.cloned.1.call-done), channel_id=1, replica_groups=mesh['dp'=8,'bank'=4] {'bank'}, use_global_device_ids=true, to_apply=%region_14.15 | all-reduce | flops 2048 | bytes 16384 | tf_op jit(solution)/shard_map/psum | solution.py:38
  213.6 0.3 multiply_reduce_fusion.1
  213.9 0.7 subtract_divide_fusion
  (6 shorter events, 0.0 us)
Async XLA Ops:
  7.2 34.5 %copy-start = (f32[512,128]{1,0:T(8,128)S(1)}, f32[512,128]{1,0:T(8,128)}, u32[]{:S(2)}) copy-start(f32[512,128]{1,0:T(8,128)} %param.6) | copy-start | bytes 786436
  7.2 98.6 %reduce-scatter.3.cloned.1.call-start = ((), (), s32[]{:S(2)}) async-start(), calls=%async_computation.2 | async-start | bytes 73728 | tf_op jit(solution)/shard_map/reduce_scatter | solution.py:39
  8.1 1.1 copy-start.1
  43.4 164.3 %reduce-scatter.5.cloned.1.call-start = ((), (), s32[]{:S(2)}) async-start(), calls=%async_computation.3 | async-start | bytes 73728 | tf_op jit(solution)/shard_map/reduce_scatter | solution.py:39
  43.5 0.7 copy-start.4
  111.9 0.7 copy-start.2
  112.8 0.7 copy-start.3
Sparse Core Ops, SparseCore 0:
  43.5 62.1 reduce-scatter.2
  147.1 60.5 reduce-scatter.4
where the time goes:
time: 222 us; the launch traced here: 221 us
  waiting for transfers between devices  99.8 us (45%)
  blocking collectives  95.9 us (43%)
  between operations  14.8 us (7%)
  matrix products  5.06 us (2%)
  other arithmetic  3.32 us (1%)
  local copies, waits for them, and re-layouts  2.43 us (1%)
    reduce_scatter x2, waiting for transfers between devices, reduce_owner(): return lax.psum_scatter(whole, 'dp', scatter_dimension=0, tiled=True)  99.7 us
    all_gather x1, blocking collectives, shards(): gathered = lax.all_gather(normed, 'dp', axis=0, tiled=True)  32.3 us
    all_gather x1, blocking collectives, shards(): gathered_grad = lax.all_gather(grad_soft, 'dp', axis=0, tiled=True)  30.5 us
    unnamed x1, blocking collectives  21.3 us
    psum x2, blocking collectives, reduce_owner(): whole = lax.psum(partials, 'bank')  11.8 us
  transfers between devices with their start and end apart: 2, of which 2 were waited for; matrix products, arithmetic and copies ran while one was open for 0% of the time, Pallas kernels for 0%

commit v1 on v0

--- a/solution.py
+++ b/solution.py
@@ -7,6 +7,21 @@
 EPSILON = 1e-06
 TAU_BACK = 0.1
 HIGHEST = lax.Precision.HIGHEST
+
+
+def show_notes(unit):
+    n_all = jax.lax.axis_size("dp")
+    small = range(n_all)
+    n_now = map(lambda w: (w, (w + 1) % n_all), small)
+    all_blocks = list(n_now)
+    t1 = [None] * n_all
+    t1[n_all - 1] = unit
+    for c in range(n_all - 2, -1, -1):
+        t1[c] = jax.lax.ppermute(t1[c + 1], "dp", all_blocks)
+    high = jnp.concatenate(t1, 0)
+    work_now = jax.lax.axis_index("dp")
+    v_now = jnp.roll(high, (work_now + 1) * unit.shape[0], 0)
+    return v_now
 
 
 def unit_rows(values):
@@ -66,7 +81,7 @@
         normed,
     )
     grad_soft, grad_local = pullback(loss_weight)
-    gathered_grad = lax.all_gather(grad_soft, "dp", axis=0, tiled=True)
+    gathered_grad = show_notes(grad_soft)
     grad_blocks = gathered_grad.reshape(-1, step_rows, width)
 
     def backward_block(paired):

time: 222 us -> 234 us (1.054)
  waiting for transfers between devices: 99.8 us -> 141 us
  blocking collectives: 95.9 us -> 65.4 us
    ppermute x0 -> x7, waiting for transfers between devices: none -> 43 us  [show_notes(): t1[c] = jax.lax.ppermute(t1[c + 1], 'dp', all_blocks)]
    all_gather x1 -> x0, blocking collectives: 30.5 us -> none  [shards(): gathered_grad = lax.all_gather(grad_soft, 'dp', axis=0, tiled=True)]
  transfers between devices with their start and end apart: 2 -> 9, of which waited for: 2 -> 9; matrix products, arithmetic and copies ran while one was open for 0% -> 0% of each run, Pallas kernels for 0% -> 0%
where the time goes in v1:
time: 234 us
  waiting for transfers between devices  141 us (60%)
  blocking collectives  65.4 us (28%)
  between operations  14.9 us (6%)
  matrix products  4.95 us (2%)
  other arithmetic  3.51 us (2%)
  local copies, waits for them, and re-layouts  2.47 us (1%)
    reduce_scatter x2, waiting for transfers between devices, reduce_owner(): return lax.psum_scatter(whole, 'dp', scatter_dimension=0, tiled=True)  98 us
    ppermute x7, waiting for transfers between devices, show_notes(): t1[c] = jax.lax.ppermute(t1[c + 1], 'dp', all_blocks)  43 us
    all_gather x1, blocking collectives, shards(): gathered = lax.all_gather(normed, 'dp', axis=0, tiled=True)  32.3 us
    unnamed x1, blocking collectives  21.3 us
    psum x2, blocking collectives, reduce_owner(): whole = lax.psum(partials, 'bank')  11.8 us
  transfers between devices with their start and end apart: 9, of which 9 were waited for; matrix products, arithmetic and copies ran while one was open for 0% of the time, Pallas kernels for 0%

profile of v1, /device:TPU:0, one launch (start us, length us, event | category | flops | bytes accessed | tf_op | source)
XLA Modules:
  0.0 233.8 jit_solution(18198492526490709803)
XLA Ops:
  7.2 0.0 copy-start
  7.2 0.0 reduce-scatter.3.cloned.1.call-start
  7.2 0.8 multiply_reduce_fusion.6
  8.1 0.0 copy-start.1
  8.1 1.1 multiply_reduce_fusion
  9.2 0.0 copy-done.1
  9.2 0.2 multiply_reduce_fusion.4
  9.4 32.3 %all_gather.3 = f32[128,128]{1,0:T(8,128)S(1)} all-gather(f32[16,128]{1,0:T(8,128)S(1)} %get-tuple-element.42), channel_id=1, replica_groups=mesh['dp'=8,'bank'=4] {'dp'}, dimensions={0}, use_global_device_ids=true | all-gather | bytes 73728 | tf_op jit(solution)/shard_map/all_gather | solution.py:64
  41.7 0.0 copy-done
  41.7 0.6 fusion.30
  42.3 1.1 fusion.27
  43.4 0.0 reduce-scatter.3.cloned.1.call-update
  43.4 0.0 reduce-scatter.5.cloned.1.call-start
  43.5 0.0 copy-start.4
  43.5 0.6 copy-done.4
  44.1 0.6 dynamic-slice.2
  45.4 21.3 %all-reduce = f32[128]{0:T(128)S(1)} all-reduce(f32[128]{0:T(128)S(1)} %get-tuple-element.47), channel_id=3, replica_groups=mesh['dp'=8,'bank'=4] {'dp'}, use_global_device_ids=true, to_apply=%region_7.8.clone | all-reduce | flops 128 | bytes 1024
  66.7 0.1 dynamic-slice.3
  66.7 39.0 %reduce-scatter.3.cloned.1.call-done = f32[16,128]{1,0:T(8,128)} async-done(((f32[128,128]{1,0:T(8,128)}), f32[16,128]{1,0:T(8,128)}) %reduce-scatter.3.cloned.1.call-update) | async-done | bytes 8208 | tf_op jit(solution)/shard_map/reduce_scatter | solution.py:54
  105.7 6.0 %all-reduce.1 = (f32[16,128]{1,0:T(8,128)S(1)}, f32[16]{0:T(128)S(1)}) all-reduce(f32[16,128]{1,0:T(8,128)} %reduce-scatter.3.cloned.1.call-done, f32[16]{0:T(128)S(1)} %dynamic-slice.3), channel_id=1, replica_groups=mesh['dp'=8,'bank'=4] {'bank'}, use_global_device_ids=true, to_apply=%region_3.0 | all-reduce | flops 2064 | bytes 16512 | tf_op jit(solution)/shard_map/psum | solution.py:53
  111.7 0.2 multiply_reduce_fusion.5
  111.9 0.0 copy-start.2
  111.9 0.7 copy-done.2
  112.6 0.2 fusion.13
  112.8 0.0 copy-start.3
  112.8 0.2 convolution_bitcast_fusion.1
  113.0 0.5 copy-done.3
  113.5 0.7 add_add_fusion
  114.2 0.1 multiply_reduce_fusion.3
  114.3 0.2 multiply_reduce_fusion.8
  114.5 0.2 convolution_add_fusion
  114.7 1.4 collective-permute-start
  116.1 4.9 %collective-permute-done = f32[16,128]{1,0:T(8,128)S(1)} collective-permute-done((f32[16,128]{1,0:T(8,128)S(1)}, f32[16,128]{1,0:T(8,128)S(1)}, u32[]{:S(2)}, u32[]{:S(2)}) %collective-permute-start) | collective-permute-done | bytes 8224 | tf_op jit(solution)/shard_map/ppermute | solution.py:20
  121.1 0.0 collective-permute-start.1
  121.1 6.3 %collective-permute-done.1 = f32[16,128]{1,0:T(8,128)S(1)} collective-permute-done((f32[16,128]{1,0:T(8,128)S(1)}, f32[16,128]{1,0:T(8,128)S(1)}, u32[]{:S(2)}, u32[]{:S(2)}) %collective-permute-start.1) | collective-permute-done | bytes 8224 | tf_op jit(solution)/shard_map/ppermute | solution.py:20
  127.4 0.0 collective-permute-start.2
  127.4 6.3 %collective-permute-done.2 = f32[16,128]{1,0:T(8,128)S(1)} collective-permute-done((f32[16,128]{1,0:T(8,128)S(1)}, f32[16,128]{1,0:T(8,128)S(1)}, u32[]{:S(2)}, u32[]{:S(2)}) %collective-permute-start.2) | collective-permute-done | bytes 8224 | tf_op jit(solution)/shard_map/ppermute | solution.py:20
  133.8 0.0 collective-permute-start.3
  133.8 6.3 %collective-permute-done.3 = f32[16,128]{1,0:T(8,128)S(1)} collective-permute-done((f32[16,128]{1,0:T(8,128)S(1)}, f32[16,128]{1,0:T(8,128)S(1)}, u32[]{:S(2)}, u32[]{:S(2)}) %collective-permute-start.3) | collective-permute-done | bytes 8224 | tf_op jit(solution)/shard_map/ppermute | solution.py:20
  140.1 0.0 collective-permute-start.4
  140.1 6.3 %collective-permute-done.4 = f32[16,128]{1,0:T(8,128)S(1)} collective-permute-done((f32[16,128]{1,0:T(8,128)S(1)}, f32[16,128]{1,0:T(8,128)S(1)}, u32[]{:S(2)}, u32[]{:S(2)}) %collective-permute-start.4) | collective-permute-done | bytes 8224 | tf_op jit(solution)/shard_map/ppermute | solution.py:20
  146.5 0.0 collective-permute-start.5
  146.5 6.3 %collective-permute-done.5 = f32[16,128]{1,0:T(8,128)S(1)} collective-permute-done((f32[16,128]{1,0:T(8,128)S(1)}, f32[16,128]{1,0:T(8,128)S(1)}, u32[]{:S(2)}, u32[]{:S(2)}) %collective-permute-start.5) | collective-permute-done | bytes 8224 | tf_op jit(solution)/shard_map/ppermute | solution.py:20
  152.8 0.0 collective-permute-start.6
  152.8 6.3 %collective-permute-done.6 = f32[16,128]{1,0:T(8,128)S(1)} collective-permute-done((f32[16,128]{1,0:T(8,128)S(1)}, f32[16,128]{1,0:T(8,128)S(1)}, u32[]{:S(2)}, u32[]{:S(2)}) %collective-permute-start.6) | collective-permute-done | bytes 8224 | tf_op jit(solution)/shard_map/ppermute | solution.py:20
  159.2 0.2 multiply_reduce_fusion.2
  159.5 0.5 convolution_multiply_fusion
  160.0 1.1 fusion.26
  161.1 0.0 reduce-scatter.5.cloned.1.call-update
  161.1 59.0 %reduce-scatter.5.cloned.1.call-done = f32[16,128]{1,0:T(8,128)} async-done(((f32[128,128]{1,0:T(8,128)}), f32[16,128]{1,0:T(8,128)}) %reduce-scatter.5.cloned.1.call-update) | async-done | bytes 8208 | tf_op jit(solution)/shard_map/reduce_scatter | solution.py:54
  220.1 5.9 %psum.26 = f32[16,128]{1,0:T(8,128)S(1)} all-reduce(f32[16,128]{1,0:T(8,128)} %reduce-scatter.5.cloned.1.call-done), channel_id=1, replica_groups=mesh['dp'=8,'bank'=4] {'bank'}, use_global_device_ids=true, to_apply=%region_14.15 | all-reduce | flops 2048 | bytes 16384 | tf_op jit(solution)/shard_map/psum | solution.py:53
  225.9 0.3 multiply_reduce_fusion.1
  226.3 0.7 subtract_divide_fusion
  (21 shorter events, 0.1 us)
Async XLA Ops:
  7.2 34.5 %copy-start = (f32[512,128]{1,0:T(8,128)S(1)}, f32[512,128]{1,0:T(8,128)}, u32[]{:S(2)}) copy-start(f32[512,128]{1,0:T(8,128)} %param.6) | copy-start | bytes 786436
  7.2 98.6 %reduce-scatter.3.cloned.1.call-start = ((), (), s32[]{:S(2)}) async-start(), calls=%async_computation.2 | async-start | bytes 73728 | tf_op jit(solution)/shard_map/reduce_scatter | solution.py:54
  8.1 1.1 copy-start.1
  43.4 176.7 %reduce-scatter.5.cloned.1.call-start = ((), (), s32[]{:S(2)}) async-start(), calls=%async_computation.3 | async-start | bytes 73728 | tf_op jit(solution)/shard_map/reduce_scatter | solution.py:54
  43.5 0.7 copy-start.4
  111.9 0.7 copy-start.2
  112.8 0.7 copy-start.3
  114.7 6.4 %collective-permute-start = (f32[16,128]{1,0:T(8,128)S(1)}, f32[16,128]{1,0:T(8,128)S(1)}, u32[]{:S(2)}, u32[]{:S(2)}) collective-permute-start(f32[16,128]{1,0:T(8,128)S(1)} %convolution_add_fusion), channel_id=1, source_target_pairs={{0,4},{4,8},{8,12},{12,16},{16,20},{20,24},{24,28},{28,0},{1,5},{5... | collective-permute-start | bytes 24584 | tf_op jit(solution)/shard_map/ppermute | solution.py:20
  121.1 6.3 %collective-permute-start.1 = (f32[16,128]{1,0:T(8,128)S(1)}, f32[16,128]{1,0:T(8,128)S(1)}, u32[]{:S(2)}, u32[]{:S(2)}) collective-permute-start(f32[16,128]{1,0:T(8,128)S(1)} %collective-permute-done), channel_id=1, source_target_pairs={{0,4},{4,8},{8,12},{12,16},{16,20},{20,24},{24,28},{28,0},{1,5},{5... | collective-permute-start | bytes 24584 | tf_op jit(solution)/shard_map/ppermute | solution.py:20
  127.4 6.3 %collective-permute-start.2 = (f32[16,128]{1,0:T(8,128)S(1)}, f32[16,128]{1,0:T(8,128)S(1)}, u32[]{:S(2)}, u32[]{:S(2)}) collective-permute-start(f32[16,128]{1,0:T(8,128)S(1)} %collective-permute-done.1), channel_id=1, source_target_pairs={{0,4},{4,8},{8,12},{12,16},{16,20},{20,24},{24,28},{28,0},{1,5},{5... | collective-permute-start | bytes 24584 | tf_op jit(solution)/shard_map/ppermute | solution.py:20
  133.8 6.3 %collective-permute-start.3 = (f32[16,128]{1,0:T(8,128)S(1)}, f32[16,128]{1,0:T(8,128)S(1)}, u32[]{:S(2)}, u32[]{:S(2)}) collective-permute-start(f32[16,128]{1,0:T(8,128)S(1)} %collective-permute-done.2), channel_id=1, source_target_pairs={{0,4},{4,8},{8,12},{12,16},{16,20},{20,24},{24,28},{28,0},{1,5},{5... | collective-permute-start | bytes 24584 | tf_op jit(solution)/shard_map/ppermute | solution.py:20
  140.1 6.3 %collective-permute-start.4 = (f32[16,128]{1,0:T(8,128)S(1)}, f32[16,128]{1,0:T(8,128)S(1)}, u32[]{:S(2)}, u32[]{:S(2)}) collective-permute-start(f32[16,128]{1,0:T(8,128)S(1)} %collective-permute-done.3), channel_id=1, source_target_pairs={{0,4},{4,8},{8,12},{12,16},{16,20},{20,24},{24,28},{28,0},{1,5},{5... | collective-permute-start | bytes 24584 | tf_op jit(solution)/shard_map/ppermute | solution.py:20
  146.5 6.3 %collective-permute-start.5 = (f32[16,128]{1,0:T(8,128)S(1)}, f32[16,128]{1,0:T(8,128)S(1)}, u32[]{:S(2)}, u32[]{:S(2)}) collective-permute-start(f32[16,128]{1,0:T(8,128)S(1)} %collective-permute-done.4), channel_id=1, source_target_pairs={{0,4},{4,8},{8,12},{12,16},{16,20},{20,24},{24,28},{28,0},{1,5},{5... | collective-permute-start | bytes 24584 | tf_op jit(solution)/shard_map/ppermute | solution.py:20
  152.8 6.3 %collective-permute-start.6 = (f32[16,128]{1,0:T(8,128)S(1)}, f32[16,128]{1,0:T(8,128)S(1)}, u32[]{:S(2)}, u32[]{:S(2)}) collective-permute-start(f32[16,128]{1,0:T(8,128)S(1)} %collective-permute-done.5), channel_id=1, source_target_pairs={{0,4},{4,8},{8,12},{12,16},{16,20},{20,24},{24,28},{28,0},{1,5},{5... | collective-permute-start | bytes 24584 | tf_op jit(solution)/shard_map/ppermute | solution.py:20
Sparse Core Ops, SparseCore 0:
  43.5 62.1 reduce-scatter.2
  161.2 58.8 reduce-scatter.4
